TPU v7x, 128 devices: a whole 4x4x4 slice. The times are simulated.
128 devices in a mesh: rows: 32 (over x_hi, y, z), text: 4 (over x_lo, core).
Axes of the slice: x: 4 (x_hi: 2, x_lo: 2; x = x_hi * 2 + x_lo), y: 4, z: 4, core: 2. Of those that a mesh axis runs over, the one named last changes fastest.
Arguments:
- image_tokens: bfloat16 [32, 512, 2048], P('rows', 'text'), may hold values from -6 to 6
- caption_embed: bfloat16 [32, 32, 4096], P('rows', 'text'), may hold values from -6 to 6
- caption_lengths: int32 [32, 2], P('rows'), may hold values from 5 to 16, as said below
- output_grad: bfloat16 [32, 512, 2048], P('rows', 'text'), may hold values from -6 to 6
- norm_self: bfloat16 [2048], P('rows'), may hold values from 0.5 to 1.5
- norm_cross: bfloat16 [2048], P('rows'), may hold values from 0.5 to 1.5
- norm_feed: bfloat16 [2048], P('rows'), may hold values from 0.5 to 1.5
- self_query: bfloat16 [2048, 2048], P('rows', 'text'), may hold values from -0.125 to 0.125
- self_key: bfloat16 [2048, 2048], P('rows', 'text'), may hold values from -0.125 to 0.125
- self_value: bfloat16 [2048, 2048], P('rows', 'text'), may hold values from -0.125 to 0.125
- self_output: bfloat16 [2048, 2048], P('text', 'rows'), may hold values from -1.5 to 1.5
- cross_query: bfloat16 [2048, 2048], P('rows', 'text'), may hold values from -0.125 to 0.125
- cross_key: bfloat16 [4096, 2048], P('rows', 'text'), may hold values from -0.09375 to 0.09375
- cross_value: bfloat16 [4096, 2048], P('rows', 'text'), may hold values from -0.09375 to 0.09375
- cross_output: bfloat16 [2048, 2048], P('text', 'rows'), may hold values from -0.375 to 0.375
- up_weight: bfloat16 [2048, 8192], P('rows', 'text'), may hold values from -0.125 to 0.125
- down_weight: bfloat16 [8192, 2048], P('text', 'rows'), may hold values from -0.0625 to 0.0625
Outputs:
- layer_output_array: bfloat16 [32, 512, 2048], P('rows', 'text')
- image_grad: float32 [32, 512, 2048], P('rows', 'text')
- caption_grad: float32 [32, 32, 4096], P('rows', 'text')
- norm_self_grad: float32 [2048], P('rows')
- norm_cross_grad: float32 [2048], P('rows')
- norm_feed_grad: float32 [2048], P('rows')
- self_query_grad: float32 [2048, 2048], P('rows', 'text')
- self_key_grad: float32 [2048, 2048], P('rows', 'text')
- self_value_grad: float32 [2048, 2048], P('rows', 'text')
- self_output_grad: float32 [2048, 2048], P('text', 'rows')
- cross_query_grad: float32 [2048, 2048], P('rows', 'text')
- cross_key_grad: float32 [4096, 2048], P('rows', 'text')
- cross_value_grad: float32 [4096, 2048], P('rows', 'text')
- cross_output_grad: float32 [2048, 2048], P('text', 'rows')
- up_grad: float32 [2048, 8192], P('rows', 'text')
- down_grad: float32 [8192, 2048], P('text', 'rows')
Inputs may be any that keep to these rules, and one draw needn't show every extreme that they name: caption_lengths[r, i] counts the live slots of image i's caption; slots at or past it are padding. Some image has 16 live slots and some has 5.
All inputs are finite; a program needn't handle non-finite values.
Results may differ from a plain program's by a relative error of at most 0.029.
Values may be sent and summed in bfloat16 or wider, within the bound.
No kernel may reach another device: no remote copies, remote signals or barrier semaphores. Data moves between devices by JAX's collectives and lax.ppermute only.
A program may use at most 192 MiB of HBM per device.

v0:
```python
import jax
import jax.numpy as jnp
from jax import lax
from jax.sharding import PartitionSpec as P

HEAD_DIM = 128
IMAGE_TOKENS = 256
PER_ROW = 2
CAP = 16
EPSILON = 1e-05


def layer_stats(resid):
    mean = jnp.mean(resid, -1, keepdims=True)
    centered = resid - mean
    inverse = lax.rsqrt(jnp.mean(centered * centered, -1, keepdims=True) + EPSILON)
    return (centered * inverse, inverse)


def norm_back(grad_norm, normed, inverse, gain):
    scaled = grad_norm * gain
    inner = (
        scaled
        - jnp.mean(scaled, -1, keepdims=True)
        - normed * jnp.mean(scaled * normed, -1, keepdims=True)
    )
    return (inverse * inner, jnp.sum(grad_norm * normed, axis=(0, 1)))


def gelu_back(hidden_pre, grad_act):
    _, pullback = jax.vjp(lambda value_in: jax.nn.gelu(value_in, approximate=False), hidden_pre)
    return pullback(grad_act)[0]


def gather_tokens(normed_low):
    return lax.all_gather(normed_low, "text", axis=1, tiled=True)


def sum_tokens(partial_value):
    return lax.psum_scatter(partial_value, "text", scatter_dimension=1, tiled=True)


def gather_grads(grad_low):
    return lax.all_gather(grad_low, "text", axis=1, tiled=True)


def sum_inputs(partial_value):
    return lax.psum_scatter(
        partial_value.astype(jnp.bfloat16), "text", scatter_dimension=1, tiled=True
    ).astype(jnp.float32)


def product(operand, factor):
    return jnp.einsum("rsd,de->rse", operand, factor, preferred_element_type=jnp.float32)


def project(operand, factor):
    return product(operand, factor).astype(jnp.bfloat16)


def product_back(operand, factor):
    return jnp.einsum("rse,de->rsd", operand, factor, preferred_element_type=jnp.float32)


def contract_product(operand, factor):
    return jnp.einsum("rsd,rse->de", operand, factor, preferred_element_type=jnp.float32)


def split_heads(value_rows, length_limit):
    return value_rows.reshape(
        value_rows.shape[0], PER_ROW, length_limit, value_rows.shape[2] // HEAD_DIM, HEAD_DIM
    )


def join_heads(value_rows):
    shape = value_rows.shape
    return value_rows.reshape(shape[0], shape[1] * shape[2], shape[3] * shape[4])


def scores_of(query_rows, key_rows):
    return jnp.einsum(
        "rbqhe,rbkhe->rbhqk", query_rows, key_rows, preferred_element_type=jnp.float32
    ) * HEAD_DIM ** (-0.5)


def attend_forward(query_rows, key_rows, value_rows, live_slots):
    scores = scores_of(query_rows, key_rows)
    if live_slots is not None:
        scores = jnp.where(live_slots, scores, -1e30)
    row_max = jnp.max(scores, -1, keepdims=True)
    shifted = jnp.exp(scores - row_max)
    row_total = jnp.sum(shifted, -1, keepdims=True)
    attention = (shifted / row_total).astype(jnp.bfloat16)
    mixed = jnp.einsum(
        "rbhqk,rbkhe->rbqhe", attention, value_rows, preferred_element_type=jnp.float32
    )
    return (mixed.astype(jnp.bfloat16), row_max + jnp.log(row_total))


def attend_back(query_rows, key_rows, value_rows, live_slots, logsum, grad_mixed):
    scores = scores_of(query_rows, key_rows)
    attention = jnp.exp(scores - logsum)
    if live_slots is not None:
        attention = jnp.where(live_slots, attention, 0.0)
    grad_values = jnp.einsum(
        "rbhqk,rbqhe->rbkhe",
        attention.astype(jnp.bfloat16),
        grad_mixed,
        preferred_element_type=jnp.float32,
    ).astype(jnp.bfloat16)
    grad_attention = jnp.einsum(
        "rbqhe,rbkhe->rbhqk", grad_mixed, value_rows, preferred_element_type=jnp.float32
    )
    row_inner = jnp.sum(attention * grad_attention, -1, keepdims=True)
    grad_scores = (attention * (grad_attention - row_inner)).astype(jnp.bfloat16)
    grad_query = (
        jnp.einsum("rbhqk,rbkhe->rbqhe", grad_scores, key_rows, preferred_element_type=jnp.float32)
        * HEAD_DIM ** (-0.5)
    ).astype(jnp.bfloat16)
    grad_keys = (
        jnp.einsum(
            "rbhqk,rbqhe->rbkhe", grad_scores, query_rows, preferred_element_type=jnp.float32
        )
        * HEAD_DIM ** (-0.5)
    ).astype(jnp.bfloat16)
    return (grad_query, grad_keys, grad_values)


def per_device(
    image_tokens,
    caption_embed,
    caption_lengths,
    output_grad,
    norm_self,
    norm_cross,
    norm_feed,
    self_query,
    self_key,
    self_value,
    self_output,
    cross_query,
    cross_key,
    cross_value,
    cross_output,
    up_weight,
    down_weight,
):
    gathered = (
        lax.all_gather(norm_self, "rows", axis=0, tiled=True),
        lax.all_gather(norm_cross, "rows", axis=0, tiled=True),
        lax.all_gather(norm_feed, "rows", axis=0, tiled=True),
        lax.all_gather(self_query, "rows", axis=0, tiled=True),
        lax.all_gather(self_key, "rows", axis=0, tiled=True),
        lax.all_gather(self_value, "rows", axis=0, tiled=True),
        lax.all_gather(self_output, "rows", axis=1, tiled=True),
        lax.all_gather(cross_query, "rows", axis=0, tiled=True),
        lax.all_gather(cross_key, "rows", axis=0, tiled=True),
        lax.all_gather(cross_value, "rows", axis=0, tiled=True),
        lax.all_gather(cross_output, "rows", axis=1, tiled=True),
        lax.all_gather(up_weight, "rows", axis=0, tiled=True),
        lax.all_gather(down_weight, "rows", axis=1, tiled=True),
    )
    gain_one = gathered[0].astype(jnp.float32)
    gain_two = gathered[1].astype(jnp.float32)
    gain_three = gathered[2].astype(jnp.float32)
    residual = image_tokens.astype(jnp.float32)
    normed_one, inverse_one = layer_stats(residual)
    first_input_tensor = gather_tokens((normed_one * gain_one).astype(jnp.bfloat16))
    query_one = split_heads(project(first_input_tensor, gathered[3]), IMAGE_TOKENS)
    key_one = split_heads(project(first_input_tensor, gathered[4]), IMAGE_TOKENS)
    value_one = split_heads(project(first_input_tensor, gathered[5]), IMAGE_TOKENS)
    mixed_one, logsum_one = attend_forward(query_one, key_one, value_one, None)
    merged_one = join_heads(mixed_one)
    residual_two = residual + sum_tokens(product(merged_one, gathered[6]))
    normed_two, inverse_two = layer_stats(residual_two)
    input_two = gather_tokens((normed_two * gain_two).astype(jnp.bfloat16))
    caption_full = lax.all_gather(caption_embed, "text", axis=1, tiled=True)
    query_two = split_heads(project(input_two, gathered[7]), IMAGE_TOKENS)
    key_two = split_heads(project(caption_full, gathered[8]), CAP)
    value_two = split_heads(project(caption_full, gathered[9]), CAP)
    slot_index = lax.broadcasted_iota(jnp.int32, (1, 1, CAP), 2)
    live_slots = (slot_index < caption_lengths[:, :, None])[:, :, None, None, :]
    mixed_two, logsum_two = attend_forward(query_two, key_two, value_two, live_slots)
    merged_two = join_heads(mixed_two)
    residual_three = residual_two + sum_tokens(product(merged_two, gathered[10]))
    normed_three, inverse_three = layer_stats(residual_three)
    input_three = gather_tokens((normed_three * gain_three).astype(jnp.bfloat16))
    hidden_pre = product(input_three, gathered[11])
    hidden_act = jax.nn.gelu(hidden_pre, approximate=False).astype(jnp.bfloat16)
    block_out = residual_three + sum_tokens(product(hidden_act, gathered[12]))
    grad_resid = output_grad.astype(jnp.float32)
    grad_full = gather_grads(grad_resid.astype(jnp.bfloat16))
    grad_down = contract_product(hidden_act, grad_full)
    grad_act = jnp.einsum(
        "rsd,fd->rsf", grad_full, gathered[12], preferred_element_type=jnp.float32
    )
    grad_pre = gelu_back(hidden_pre, grad_act).astype(jnp.bfloat16)
    grad_up = contract_product(input_three, grad_pre)
    grad_norm = sum_inputs(product_back(grad_pre, gathered[11]))
    grad_input, feed_gain_grad = norm_back(grad_norm, normed_three, inverse_three, gain_three)
    grad_resid = grad_resid + grad_input
    grad_full = gather_grads(grad_resid.astype(jnp.bfloat16))
    grad_cout = contract_product(merged_two, grad_full)
    grad_merged = jnp.einsum(
        "rsd,ed->rse", grad_full, gathered[10], preferred_element_type=jnp.float32
    ).astype(jnp.bfloat16)
    cross_gq, cross_gk, cross_gv = attend_back(
        query_two,
        key_two,
        value_two,
        live_slots,
        logsum_two,
        split_heads(grad_merged, IMAGE_TOKENS),
    )
    cross_gq = join_heads(cross_gq)
    cross_gk = join_heads(cross_gk)
    cross_gv = join_heads(cross_gv)
    grad_cquery = contract_product(input_two, cross_gq)
    grad_ckey = contract_product(caption_full, cross_gk)
    grad_cvalue = contract_product(caption_full, cross_gv)
    caption_grad = lax.psum_scatter(
        (product_back(cross_gk, gathered[8]) + product_back(cross_gv, gathered[9])).astype(
            jnp.bfloat16
        ),
        "text",
        scatter_dimension=1,
        tiled=True,
    ).astype(jnp.float32)
    grad_norm = sum_inputs(product_back(cross_gq, gathered[7]))
    grad_input, cross_gain_grad = norm_back(grad_norm, normed_two, inverse_two, gain_two)
    grad_resid = grad_resid + grad_input
    grad_full = gather_grads(grad_resid.astype(jnp.bfloat16))
    grad_sout = contract_product(merged_one, grad_full)
    grad_merged = jnp.einsum(
        "rsd,ed->rse", grad_full, gathered[6], preferred_element_type=jnp.float32
    ).astype(jnp.bfloat16)
    self_gq, self_key_gradient_part, self_gv = attend_back(
        query_one, key_one, value_one, None, logsum_one, split_heads(grad_merged, IMAGE_TOKENS)
    )
    self_gq = join_heads(self_gq)
    self_key_gradient_part = join_heads(self_key_gradient_part)
    self_gv = join_heads(self_gv)
    grad_squery = contract_product(first_input_tensor, self_gq)
    self_attention_key_gradient = contract_product(first_input_tensor, self_key_gradient_part)
    grad_svalue = contract_product(first_input_tensor, self_gv)
    grad_norm = sum_inputs(
        product_back(self_gq, gathered[3])
        + product_back(self_key_gradient_part, gathered[4])
        + product_back(self_gv, gathered[5])
    )
    grad_input, self_norm_gain_gradient = norm_back(grad_norm, normed_one, inverse_one, gain_one)
    grad_resid = grad_resid + grad_input
    gain_totals = lax.psum((self_norm_gain_gradient, cross_gain_grad, feed_gain_grad), "text")
    results = (
        lax.psum_scatter(
            gain_totals[0].astype(jnp.bfloat16), "rows", scatter_dimension=0, tiled=True
        ).astype(jnp.float32),
        lax.psum_scatter(
            gain_totals[1].astype(jnp.bfloat16), "rows", scatter_dimension=0, tiled=True
        ).astype(jnp.float32),
        lax.psum_scatter(
            gain_totals[2].astype(jnp.bfloat16), "rows", scatter_dimension=0, tiled=True
        ).astype(jnp.float32),
        lax.psum_scatter(
            grad_squery.astype(jnp.bfloat16), "rows", scatter_dimension=0, tiled=True
        ).astype(jnp.float32),
        lax.psum_scatter(
            self_attention_key_gradient.astype(jnp.bfloat16),
            "rows",
            scatter_dimension=0,
            tiled=True,
        ).astype(jnp.float32),
        lax.psum_scatter(
            grad_svalue.astype(jnp.bfloat16), "rows", scatter_dimension=0, tiled=True
        ).astype(jnp.float32),
        lax.psum_scatter(
            grad_sout.astype(jnp.bfloat16), "rows", scatter_dimension=1, tiled=True
        ).astype(jnp.float32),
        lax.psum_scatter(
            grad_cquery.astype(jnp.bfloat16), "rows", scatter_dimension=0, tiled=True
        ).astype(jnp.float32),
        lax.psum_scatter(
            grad_ckey.astype(jnp.bfloat16), "rows", scatter_dimension=0, tiled=True
        ).astype(jnp.float32),
        lax.psum_scatter(
            grad_cvalue.astype(jnp.bfloat16), "rows", scatter_dimension=0, tiled=True
        ).astype(jnp.float32),
        lax.psum_scatter(
            grad_cout.astype(jnp.bfloat16), "rows", scatter_dimension=1, tiled=True
        ).astype(jnp.float32),
        lax.psum_scatter(
            grad_up.astype(jnp.bfloat16), "rows", scatter_dimension=0, tiled=True
        ).astype(jnp.float32),
        lax.psum_scatter(
            grad_down.astype(jnp.bfloat16), "rows", scatter_dimension=1, tiled=True
        ).astype(jnp.float32),
    )
    return (
        block_out.astype(jnp.bfloat16),
        grad_resid,
        caption_grad,
        results[0],
        results[1],
        results[2],
        results[3],
        results[4],
        results[5],
        results[6],
        results[7],
        results[8],
        results[9],
        results[10],
        results[11],
        results[12],
    )


def solution(mesh):
    in_specs = (
        P("rows", "text", None),
        P("rows", "text", None),
        P("rows", None),
        P("rows", "text", None),
        P("rows"),
        P("rows"),
        P("rows"),
        P("rows", "text"),
        P("rows", "text"),
        P("rows", "text"),
        P("text", "rows"),
        P("rows", "text"),
        P("rows", "text"),
        P("rows", "text"),
        P("text", "rows"),
        P("rows", "text"),
        P("text", "rows"),
    )
    out_specs = (
        P("rows", "text", None),
        P("rows", "text", None),
        P("rows", "text", None),
        P("rows"),
        P("rows"),
        P("rows"),
        P("rows", "text"),
        P("rows", "text"),
        P("rows", "text"),
        P("text", "rows"),
        P("rows", "text"),
        P("rows", "text"),
        P("rows", "text"),
        P("text", "rows"),
        P("rows", "text"),
        P("text", "rows"),
    )
    return jax.shard_map(
        per_device, mesh=mesh, in_specs=in_specs, out_specs=out_specs, check_vma=False
    )
```

profile of v0, /device:TPU:0, one launch (start us, length us, event | category | flops | bytes accessed | tf_op | source)
XLA Modules:
  0.0 3408.7 jit_solution(11320915709437666502)
XLA Ops:
  14.3 185.2 %all-reduce.8 = (bf16[2048]{0:T(1024)(128)(2,1)S(1)}, bf16[2048]{0:T(1024)(128)(2,1)S(1)}, bf16[2048]{0:T(1024)(128)(2,1)}) all-reduce(bf16[2048]{0:T(1024)(128)(2,1)S(1)} %dynamic-update-slice, bf16[2048]{0:T(1024)(128)(2,1)S(1)} %dynamic-update-slice.1, ...), channel_id=1, replica_groups=mesh['rows'=32,'text'=4] {'rows'}, use_global_device_ids=true, to_apply=%add | all-reduce | flops 6144 | bytes 24576
  204.5 20.8 all-gather.17.cloned.1.call-done
  225.3 75.0 %all-gather.21.cloned.1.call-done = bf16[2048,512]{1,0:T(8,128)(2,1)} async-done(((bf16[64,512]{1,0:T(8,128)(2,1)}), bf16[2048,512]{1,0:T(8,128)(2,1)}) %all-gather.21.cloned.1.call-update) | async-done | bytes 2097168 | tf_op jit(solution)/shard_map/all_gather | solution.py:152
  300.3 3.5 fusion.56
  304.1 68.2 %all-gather.23.cloned.1.call-done = bf16[2048,512]{1,0:T(8,128)(2,1)} async-done(((bf16[64,512]{1,0:T(8,128)(2,1)}), bf16[2048,512]{1,0:T(8,128)(2,1)}) %all-gather.23.cloned.1.call-update) | async-done | bytes 2097168 | tf_op jit(solution)/shard_map/all_gather | solution.py:153
  372.4 3.5 fusion.59
  376.3 68.1 %all-gather.19.cloned.1.call-done = bf16[2048,512]{1,0:T(8,128)(2,1)} async-done(((bf16[64,512]{1,0:T(8,128)(2,1)}), bf16[2048,512]{1,0:T(8,128)(2,1)}) %all-gather.19.cloned.1.call-update) | async-done | bytes 2097168 | tf_op jit(solution)/shard_map/all_gather | solution.py:154
  444.3 3.5 fusion.53
  451.3 65.0 %all-gather.25.cloned.1.call-done = bf16[512,2048]{0,1:T(8,128)(2,1)} async-done(((bf16[512,64]{0,1:T(8,128)(2,1)}), bf16[512,2048]{0,1:T(8,128)(2,1)}) %all-gather.25.cloned.1.call-update) | async-done | bytes 2097168 | tf_op jit(solution)/shard_map/all_gather | solution.py:155
  516.3 4.9 convolution_bitcast_fusion.1
  523.5 41.4 %reduce-scatter.22.cloned.1.call-done = f32[1,128,2048]{2,1,0:T(8,128)} async-done(((f32[1,512,2048]{2,1,0:T(8,128)}), f32[1,128,2048]{2,1,0:T(8,128)}) %reduce-scatter.22.cloned.1.call-update) | async-done | bytes 1048592 | tf_op jit(solution)/shard_map/reduce_scatter | solution.py:40
  568.5 6.0 all_gather.66
  574.6 75.4 %all-gather.33.cloned.1.call-done = bf16[4096,512]{1,0:T(8,128)(2,1)} async-done(((bf16[128,512]{1,0:T(8,128)(2,1)}), bf16[4096,512]{1,0:T(8,128)(2,1)}) %all-gather.33.cloned.1.call-update) | async-done | bytes 4194320 | tf_op jit(solution)/shard_map/all_gather | solution.py:157
  650.0 3.0 convolution_convert_fusion.16
  653.6 79.3 %all-gather.27.cloned.1.call-done = bf16[4096,512]{1,0:T(8,128)(2,1)} async-done(((bf16[128,512]{1,0:T(8,128)(2,1)}), bf16[4096,512]{1,0:T(8,128)(2,1)}) %all-gather.27.cloned.1.call-update) | async-done | bytes 4194320 | tf_op jit(solution)/shard_map/all_gather | solution.py:158
  732.9 3.0 convolution_convert_fusion.17
  736.6 69.6 %all-gather.31.cloned.1.call-done = bf16[2048,512]{1,0:T(8,128)(2,1)} async-done(((bf16[64,512]{1,0:T(8,128)(2,1)}), bf16[2048,512]{1,0:T(8,128)(2,1)}) %all-gather.31.cloned.1.call-update) | async-done | bytes 2097168 | tf_op jit(solution)/shard_map/all_gather | solution.py:156
  806.1 29.3 all-gather.29.cloned.1.call-done
  835.5 4.3 fusion.62
  848.2 62.7 %all-gather.35.cloned.1.call-done = bf16[512,2048]{0,1:T(8,128)(2,1)} async-done(((bf16[512,64]{0,1:T(8,128)(2,1)}), bf16[512,2048]{0,1:T(8,128)(2,1)}) %all-gather.35.cloned.1.call-update) | async-done | bytes 2097168 | tf_op jit(solution)/shard_map/all_gather | solution.py:159
  910.9 5.1 convolution_bitcast_fusion
  917.5 42.2 %reduce-scatter.24.cloned.1.call-done = f32[1,128,2048]{2,1,0:T(8,128)} async-done(((f32[1,512,2048]{2,1,0:T(8,128)}), f32[1,128,2048]{2,1,0:T(8,128)}) %reduce-scatter.24.cloned.1.call-update) | async-done | bytes 1048592 | tf_op jit(solution)/shard_map/reduce_scatter | solution.py:40
  964.8 102.8 %all-gather.39.cloned.1.call-done = bf16[2048,2048]{1,0:T(8,128)(2,1)} async-done(((bf16[64,2048]{1,0:T(8,128)(2,1)}), bf16[2048,2048]{1,0:T(8,128)(2,1)}) %all-gather.39.cloned.1.call-update) | async-done | bytes 8388624 | tf_op jit(solution)/shard_map/all_gather | solution.py:160
  1067.7 29.0 all-gather.37.cloned.1.call-done
  1096.7 18.3 multiply_convert_fusion
  1115.0 13.2 all-gather.43.cloned.1.call-done
  1128.2 107.9 %all-gather.41.cloned.1.call-done = bf16[2048,2048]{0,1:T(8,128)(2,1)} async-done(((bf16[2048,64]{0,1:T(8,128)(2,1)}), bf16[2048,2048]{0,1:T(8,128)(2,1)}) %all-gather.41.cloned.1.call-update) | async-done | bytes 8388624 | tf_op jit(solution)/shard_map/all_gather | solution.py:161
  1236.1 12.0 add_convert_fusion.1
  1249.5 6.2 fusion.10
  1255.8 10.5 convolution_bitcast_fusion.2
  1266.4 15.6 reduce-scatter.28.cloned.1.call-done
  1285.0 45.8 %reduce-scatter.26.cloned.1.call-done = f32[1,128,2048]{2,1,0:T(8,128)} async-done(((f32[1,512,2048]{2,1,0:T(8,128)}), f32[1,128,2048]{2,1,0:T(8,128)}) %reduce-scatter.26.cloned.1.call-update) | async-done | bytes 1048592 | tf_op jit(solution)/shard_map/reduce_scatter | solution.py:40
  1330.7 3.9 fusion.171
  1335.5 29.3 all-gather.45.cloned.1.call-done
  1364.7 4.3 fusion.65
  1377.7 4.4 fusion.12
  1382.1 29.3 reduce-scatter.30.cloned.1.call-done
  1413.6 3.0 fusion.169
  1419.6 3.6 fusion.155
  1425.3 4.4 convolution_convert_fusion.4
  1429.8 4.2 convolution_convert_fusion.5
  1434.0 10.1 convolution_convert_fusion
  1444.4 10.0 convolution_convert_fusion.1
  1454.5 3.3 fusion.1
  1457.8 6.5 copy.121
  1465.1 3.3 fusion
  1468.4 6.6 copy.119
  1476.0 4.3 convolution_convert_fusion.6
  1480.6 3.5 fusion.68
  1491.0 4.4 convolution_convert_fusion.8
  1499.7 4.3 convolution_convert_fusion.9
  1506.8 3.0 fusion.107
  1519.2 139.2 %reduce-scatter.46.cloned.1.call-done = bf16[512,64]{0,1:T(8,128)(2,1)} async-done(((bf16[512,2048]{0,1:T(8,128)(2,1)}), bf16[512,64]{0,1:T(8,128)(2,1)}) %reduce-scatter.46.cloned.1.call-update) | async-done | bytes 65552 | tf_op jit(solution)/shard_map/reduce_scatter | solution.py:288
  1659.9 182.9 %reduce-scatter.44.cloned.1.call-done = bf16[64,512]{1,0:T(8,128)(2,1)} async-done(((bf16[2048,512]{1,0:T(8,128)(2,1)}), bf16[64,512]{1,0:T(8,128)(2,1)}) %reduce-scatter.44.cloned.1.call-update) | async-done | bytes 65552 | tf_op jit(solution)/shard_map/reduce_scatter | solution.py:279
  1844.3 198.5 %reduce-scatter.50.cloned.1.call-done = bf16[2048,64]{0,1:T(8,128)(2,1)} async-done(((bf16[2048,2048]{0,1:T(8,128)(2,1)}), bf16[2048,64]{0,1:T(8,128)(2,1)}) %reduce-scatter.50.cloned.1.call-update) | async-done | bytes 262160 | tf_op jit(solution)/shard_map/reduce_scatter | solution.py:294
  2044.6 198.3 %reduce-scatter.48.cloned.1.call-done = bf16[64,2048]{1,0:T(8,128)(2,1)} async-done(((bf16[2048,2048]{1,0:T(8,128)(2,1)}), bf16[64,2048]{1,0:T(8,128)(2,1)}) %reduce-scatter.48.cloned.1.call-update) | async-done | bytes 262160 | tf_op jit(solution)/shard_map/reduce_scatter | solution.py:291
  2244.7 187.7 %reduce-scatter.54.cloned.1.call-done = bf16[128,512]{1,0:T(8,128)(2,1)} async-done(((bf16[4096,512]{1,0:T(8,128)(2,1)}), bf16[128,512]{1,0:T(8,128)(2,1)}) %reduce-scatter.54.cloned.1.call-update) | async-done | bytes 131088
  2434.3 187.5 %reduce-scatter.52.cloned.1.call-done = bf16[128,512]{1,0:T(8,128)(2,1)} async-done(((bf16[4096,512]{1,0:T(8,128)(2,1)}), bf16[128,512]{1,0:T(8,128)(2,1)}) %reduce-scatter.52.cloned.1.call-update) | async-done | bytes 131088
  2623.7 182.4 %reduce-scatter.42.cloned.1.call-done = bf16[512,64]{0,1:T(8,128)(2,1)} async-done(((bf16[512,2048]{0,1:T(8,128)(2,1)}), bf16[512,64]{0,1:T(8,128)(2,1)}) %reduce-scatter.42.cloned.1.call-update) | async-done | bytes 65552 | tf_op jit(solution)/shard_map/reduce_scatter | solution.py:276
  2807.5 182.7 %reduce-scatter.38.cloned.1.call-done = bf16[64,512]{1,0:T(8,128)(2,1)} async-done(((bf16[2048,512]{1,0:T(8,128)(2,1)}), bf16[64,512]{1,0:T(8,128)(2,1)}) %reduce-scatter.38.cloned.1.call-update) | async-done | bytes 65552 | tf_op jit(solution)/shard_map/reduce_scatter | solution.py:267
  2991.7 182.8 %reduce-scatter.36.cloned.1.call-done = bf16[64,512]{1,0:T(8,128)(2,1)} async-done(((bf16[2048,512]{1,0:T(8,128)(2,1)}), bf16[64,512]{1,0:T(8,128)(2,1)}) %reduce-scatter.36.cloned.1.call-update) | async-done | bytes 65552 | tf_op jit(solution)/shard_map/reduce_scatter | solution.py:264
  3176.0 24.0 reduce-scatter.32.cloned.1.call-done
  3201.5 10.3 all-reduce.6
  3211.8 183.9 %all-reduce.7 = (bf16[2048]{0:T(1024)(128)(2,1)S(1)}, bf16[2048]{0:T(1024)(128)(2,1)S(1)}, bf16[2048]{0:T(1024)(128)(2,1)S(1)}) all-reduce(bf16[2048]{0:T(1024)(128)(2,1)S(1)} %get-tuple-element.73, bf16[2048]{0:T(1024)(128)(2,1)S(1)} %get-tuple-element.74, ...), channel_id=9, replica_groups=mesh['rows'=32,'text'=4] {'rows'}, use_global_device_ids=true, to_apply=%region_27.28.clone | all-reduce | flops 6144 | bytes 24576
  (255 shorter events, 105.8 us)
Async XLA Ops:
  7.2 218.1 %all-gather.17.cloned.1.call-start = ((), (), s32[]{:S(2)}) async-start(), calls=%async_computation.17 | async-start | bytes 2621440 | tf_op jit(solution)/shard_map/all_gather | solution.py:36
  8.4 216.9 %copy-start.36 = (f32[128]{0:T(128)}, f32[128]{0:T(128)S(1)}, u32[]{:S(2)}) copy-start(f32[128]{0:T(128)S(1)} %broadcast_multiply_fusion.8) | copy-start | bytes 1540
  9.8 215.5 %copy-start.40 = (f32[128]{0:T(128)}, f32[128]{0:T(128)S(1)}, u32[]{:S(2)}) copy-start(f32[128]{0:T(128)S(1)} %add_rsqrt_fusion.2) | copy-start | bytes 1540
  199.5 25.8 copy-start.23
  201.8 98.5 %all-gather.21.cloned.1.call-start = ((), (), s32[]{:S(2)}) async-start(), calls=%async_computation.19 | async-start | bytes 2162688 | tf_op jit(solution)/shard_map/all_gather | solution.py:152
  202.5 169.9 %all-gather.23.cloned.1.call-start = ((), (), s32[]{:S(2)}) async-start(), calls=%async_computation.20 | async-start | bytes 2162688 | tf_op jit(solution)/shard_map/all_gather | solution.py:153
  203.3 241.1 %all-gather.19.cloned.1.call-start = ((), (), s32[]{:S(2)}) async-start(), calls=%async_computation.18 | async-start | bytes 2162688 | tf_op jit(solution)/shard_map/all_gather | solution.py:154
  203.8 312.5 %all-gather.25.cloned.1.call-start = ((), (), s32[]{:S(2)}) async-start(), calls=%async_computation.21 | async-start | bytes 2162688 | tf_op jit(solution)/shard_map/all_gather | solution.py:155
  204.4 360.5 %reduce-scatter.22.cloned.1.call-start = ((), (), s32[]{:S(2)}) async-start(), calls=%async_computation.22 | async-start | bytes 5242880 | tf_op jit(solution)/shard_map/reduce_scatter | solution.py:40
  304.1 144.6 %copy-start.6 = (bf16[2,256,4,128]{1,3,2,0:T(8,128)(2,1)}, bf16[2,256,4,128]{1,3,2,0:T(8,128)(2,1)S(1)}, u32[]{:S(2)}) copy-start(bf16[2,256,4,128]{1,3,2,0:T(8,128)(2,1)S(1)} %copy.103) | copy-start | bytes 1572868
  376.3 72.5 %copy-start.5 = (bf16[2,256,4,128]{1,3,2,0:T(8,128)(2,1)}, bf16[2,256,4,128]{1,3,2,0:T(8,128)(2,1)S(1)}, u32[]{:S(2)}) copy-start(bf16[2,256,4,128]{1,3,2,0:T(8,128)(2,1)S(1)} %copy.100) | copy-start | bytes 1572868
  451.3 69.8 %copy-start.17 = (bf16[1,2,256,4,128]{4,3,2,1,0:T(4,128)(2,1)}, bf16[1,2,256,4,128]{4,3,2,1,0:T(4,128)(2,1)S(1)}, u32[]{:S(2)}) copy-start(bf16[1,2,256,4,128]{4,3,2,1,0:T(4,128)(2,1)S(1)} %copy.89) | copy-start | bytes 1572868
  521.2 47.4 %copy-start.29 = (bf16[1,8,4096]{2,1,0:T(8,128)(2,1)S(1)}, bf16[1,8,4096]{2,1,0:T(8,128)(2,1)}, u32[]{:S(2)}) copy-start(bf16[1,8,4096]{2,1,0:T(8,128)(2,1)} %param.18) | copy-start | bytes 196612
  521.2 53.3 %copy-start.45 = (s32[1,2]{1,0:T(1,128)S(1)}, s32[1,2]{1,0:T(1,128)}, u32[]{:S(2)}) copy-start(s32[1,2]{1,0:T(1,128)} %param.19) | copy-start | bytes 28
  521.2 128.8 %all-gather.33.cloned.1.call-start = ((), (), s32[]{:S(2)}) async-start(), calls=%async_computation.26 | async-start | bytes 4325376 | tf_op jit(solution)/shard_map/all_gather | solution.py:157
  522.0 211.0 %all-gather.27.cloned.1.call-start = ((), (), s32[]{:S(2)}) async-start(), calls=%async_computation.23 | async-start | bytes 4325376 | tf_op jit(solution)/shard_map/all_gather | solution.py:158
  522.7 283.4 %all-gather.31.cloned.1.call-start = ((), (), s32[]{:S(2)}) async-start(), calls=%async_computation.25 | async-start | bytes 2162688 | tf_op jit(solution)/shard_map/all_gather | solution.py:156
  523.4 312.0 %all-gather.29.cloned.1.call-start = ((), (), s32[]{:S(2)}) async-start(), calls=%async_computation.24 | async-start | bytes 2621440 | tf_op jit(solution)/shard_map/all_gather | solution.py:36
  566.4 169.5 %copy-start.38 = (f32[128]{0:T(128)}, f32[128]{0:T(128)S(1)}, u32[]{:S(2)}) copy-start(f32[128]{0:T(128)S(1)} %broadcast_multiply_fusion.7) | copy-start | bytes 1540
  566.7 169.2 %copy-start.42 = (f32[128]{0:T(128)}, f32[128]{0:T(128)S(1)}, u32[]{:S(2)}) copy-start(f32[128]{0:T(128)S(1)} %add_rsqrt_fusion.1) | copy-start | bytes 1540
  567.7 343.2 %all-gather.35.cloned.1.call-start = ((), (), s32[]{:S(2)}) async-start(), calls=%async_computation.27 | async-start | bytes 2162688 | tf_op jit(solution)/shard_map/all_gather | solution.py:159
  568.5 391.2 %reduce-scatter.24.cloned.1.call-start = ((), (), s32[]{:S(2)}) async-start(), calls=%async_computation.28 | async-start | bytes 5242880 | tf_op jit(solution)/shard_map/reduce_scatter | solution.py:40
  574.6 268.5 %copy-start.35 = (pred[2,16]{1,0:T(4,128)(4,1)}, pred[2,16]{1,0:T(4,128)(4,1)S(1)}, u32[]{:S(2)}) copy-start(pred[2,16]{1,0:T(4,128)(4,1)S(1)} %iota_compare_fusion) | copy-start | bytes 100
  916.0 151.7 %all-gather.39.cloned.1.call-start = ((), (), s32[]{:S(2)}) async-start(), calls=%async_computation.30 | async-start | bytes 8650752 | tf_op jit(solution)/shard_map/all_gather | solution.py:160
  916.8 179.9 %all-gather.37.cloned.1.call-start = ((), (), s32[]{:S(2)}) async-start(), calls=%async_computation.29 | async-start | bytes 2621440 | tf_op jit(solution)/shard_map/all_gather | solution.py:36
  963.6 164.5 %all-gather.43.cloned.1.call-start = ((), (), s32[]{:S(2)}) async-start(), calls=%async_computation.33 | async-start | bytes 2621440 | tf_op jit(solution)/shard_map/all_gather | solution.py:44
  964.2 271.9 %all-gather.41.cloned.1.call-start = ((), (), s32[]{:S(2)}) async-start(), calls=%async_computation.31 | async-start | bytes 8650752 | tf_op jit(solution)/shard_map/all_gather | solution.py:161
  964.8 317.2 %reduce-scatter.28.cloned.1.call-start = ((), (), s32[]{:S(2)}) async-start(), calls=%async_computation.34 | async-start | bytes 2621440 | tf_op jit(solution)/shard_map/reduce_scatter | solution.py:48
  1236.1 13.4 copy-start.43
  1255.7 75.0 %reduce-scatter.26.cloned.1.call-start = ((), (), s32[]{:S(2)}) async-start(), calls=%async_computation.32 | async-start | bytes 5242880 | tf_op jit(solution)/shard_map/reduce_scatter | solution.py:40
  1266.3 98.4 %all-gather.45.cloned.1.call-start = ((), (), s32[]{:S(2)}) async-start(), calls=%async_computation.35 | async-start | bytes 2621440 | tf_op jit(solution)/shard_map/all_gather | solution.py:44
  1334.7 76.8 %reduce-scatter.30.cloned.1.call-start = ((), (), s32[]{:S(2)}) async-start(), calls=%async_computation.36 | async-start | bytes 2621440 | tf_op jit(solution)/shard_map/reduce_scatter | solution.py:48
  1382.1 93.0 %all-gather.47.cloned.1.call-start = ((), (), s32[]{:S(2)}) async-start(), calls=%async_computation.37 | async-start | bytes 2621440 | tf_op jit(solution)/shard_map/all_gather | solution.py:44
  1416.6 101.1 %reduce-scatter.34.cloned.1.call-start = ((), (), s32[]{:S(2)}) async-start(), calls=%async_computation.39 | async-start | bytes 327680 | tf_op jit(solution)/shard_map/reduce_scatter | solution.py:221
  1416.8 6.4 copy-start.2
  1418.2 4.9 copy-start.21
  1419.6 5.7 copy-start.19
  1425.2 4.5 copy-start.20
  1425.2 233.2 %reduce-scatter.46.cloned.1.call-start = ((), (), s32[]{:S(2)}) async-start(), calls=%async_computation.45 | async-start | bytes 2162688 | tf_op jit(solution)/shard_map/reduce_scatter | solution.py:288
  1429.7 413.1 %reduce-scatter.44.cloned.1.call-start = ((), (), s32[]{:S(2)}) async-start(), calls=%async_computation.44 | async-start | bytes 2162688 | tf_op jit(solution)/shard_map/reduce_scatter | solution.py:279
  1434.0 608.9 %reduce-scatter.50.cloned.1.call-start = ((), (), s32[]{:S(2)}) async-start(), calls=%async_computation.47 | async-start | bytes 8650752 | tf_op jit(solution)/shard_map/reduce_scatter | solution.py:294
  1444.2 798.8 %reduce-scatter.48.cloned.1.call-start = ((), (), s32[]{:S(2)}) async-start(), calls=%async_computation.46 | async-start | bytes 8650752 | tf_op jit(solution)/shard_map/reduce_scatter | solution.py:291
  1454.5 978.0 %reduce-scatter.54.cloned.1.call-start = ((), (), s32[]{:S(2)}) async-start(), calls=%async_computation.49 | async-start | bytes 4325376
  1464.4 1157.5 %reduce-scatter.52.cloned.1.call-start = ((), (), s32[]{:S(2)}) async-start(), calls=%async_computation.48 | async-start | bytes 4325376
  1475.0 5.6 copy-start.26
  1475.0 5.6 copy-start.31
  1475.0 1331.0 %reduce-scatter.42.cloned.1.call-start = ((), (), s32[]{:S(2)}) async-start(), calls=%async_computation.43 | async-start | bytes 2162688 | tf_op jit(solution)/shard_map/reduce_scatter | solution.py:276
  1480.3 1509.9 %reduce-scatter.38.cloned.1.call-start = ((), (), s32[]{:S(2)}) async-start(), calls=%async_computation.41 | async-start | bytes 2162688 | tf_op jit(solution)/shard_map/reduce_scatter | solution.py:267
  1480.6 5.7 copy-start.14
  1495.4 1679.1 %reduce-scatter.36.cloned.1.call-start = ((), (), s32[]{:S(2)}) async-start(), calls=%async_computation.40 | async-start | bytes 2162688 | tf_op jit(solution)/shard_map/reduce_scatter | solution.py:264
  1499.7 4.4 copy-start.4
  1504.0 2.8 copy-start.9
  1504.1 1695.9 %reduce-scatter.32.cloned.1.call-start = ((), (), s32[]{:S(2)}) async-start(), calls=%async_computation.38 | async-start | bytes 2621440 | tf_op jit(solution)/shard_map/reduce_scatter | solution.py:48
  1506.8 3.1 copy-start.11
  1506.8 3.1 copy-start.15
  1511.5 2.7 copy-start.44
  1514.1 1883.3 %reduce-scatter.40.cloned.1.call-start = ((), (), s32[]{:S(2)}) async-start(), calls=%async_computation.42 | async-start | bytes 2162688 | tf_op jit(solution)/shard_map/reduce_scatter | solution.py:273
  1516.8 1683.2 %copy-start.1 = (bf16[1,128,2048]{2,1,0:T(8,128)(2,1)S(1)}, bf16[1,128,2048]{2,1,0:T(8,128)(2,1)}, u32[]{:S(2)}) copy-start(bf16[1,128,2048]{2,1,0:T(8,128)(2,1)} %param.17) | copy-start | bytes 1572868
  1516.8 1683.2 %copy-start.24 = (f32[2048]{0:T(1024)S(1)}, f32[2048]{0:T(1024)}, u32[]{:S(2)}) copy-start(f32[2048]{0:T(1024)} %copy-done.23) | copy-start | bytes 24580
  1516.8 1683.2 %copy-start.37 = (f32[128]{0:T(128)S(1)}, f32[128]{0:T(128)}, u32[]{:S(2)}) copy-start(f32[128]{0:T(128)} %copy-done.36) | copy-start | bytes 1540
  1516.8 1683.2 %copy-start.41 = (f32[128]{0:T(128)S(1)}, f32[128]{0:T(128)}, u32[]{:S(2)}) copy-start(f32[128]{0:T(128)} %copy-done.40) | copy-start | bytes 1540
  1516.8 1684.7 %copy-start.32 = (f32[2048]{0:T(1024)S(1)}, f32[2048]{0:T(1024)}, u32[]{:S(2)}) copy-start(f32[2048]{0:T(1024)} %get-tuple-element.64) | copy-start | bytes 24580
  1516.8 1684.7 %copy-start.33 = (f32[2048]{0:T(1024)S(1)}, f32[2048]{0:T(1024)}, u32[]{:S(2)}) copy-start(f32[2048]{0:T(1024)} %get-tuple-element.66) | copy-start | bytes 24580
  1516.9 1882.1 %copy-start.8 = (f32[1,128,2048]{2,1,0:T(8,128)S(1)}, f32[1,128,2048]{2,1,0:T(8,128)}, u32[]{:S(2)}) copy-start(f32[1,128,2048]{2,1,0:T(8,128)} %get-tuple-element.83) | copy-start | bytes 3145732
  (16 other events, 14.8 us)
Sparse Core Ops, SparseCore 0:
  201.9 23.3 all-gather.16
  228.5 71.7 all-gather.20
  303.4 68.9 all-gather.22
  375.4 68.9 all-gather.18
  447.4 68.9 all-gather.24
  521.3 43.5 reduce-scatter.21
  568.5 81.4 all-gather.32
  653.6 79.2 all-gather.26
  736.6 69.5 all-gather.30
  808.3 27.1 all-gather.28
  839.1 71.7 all-gather.34
  916.1 43.5 reduce-scatter.23
  962.9 104.7 all-gather.38
  1069.8 26.8 all-gather.36
  1098.2 29.9 all-gather.42
  1131.2 104.8 all-gather.40
  1255.9 26.1 reduce-scatter.27
  1284.4 46.2 reduce-scatter.25
  1334.8 29.8 all-gather.44
  1382.2 29.2 reduce-scatter.29
  1416.7 29.8 all-gather.46
  1449.7 18.2 reduce-scatter.33
  1470.4 188.0 reduce-scatter.45
  1660.8 182.0 reduce-scatter.43
  1845.2 197.5 reduce-scatter.49
  2045.1 197.7 reduce-scatter.47
  2245.2 187.2 reduce-scatter.53
  2434.8 186.9 reduce-scatter.51
  2624.2 181.7 reduce-scatter.41
  2808.4 181.7 reduce-scatter.37
  2992.6 181.8 reduce-scatter.35
  3177.1 22.8 reduce-scatter.31
  3202.2 188.5 reduce-scatter.39
where the time goes:
time: 3420 us; the launch traced here: 3410 us
  waiting for transfers between devices  2740 us (80%)
  blocking collectives  385 us (11%)
  matrix products  169 us (5%)
  local copies, waits for them, and re-layouts  47 us (1%)
  other arithmetic  45.3 us (1%)
    unnamed x35, waiting for transfers between devices  383 us
    unnamed x2, blocking collectives  369 us
    reduce_scatter x1, waiting for transfers between devices, per_device(): lax.psum_scatter(grad_down.astype(jnp.bfloat16), 'rows', scatter_dimensio...  199 us
    reduce_scatter x1, waiting for transfers between devices, per_device(): lax.psum_scatter(grad_up.astype(jnp.bfloat16), 'rows', scatter_dimension=...  198 us
    reduce_scatter x1, waiting for transfers between devices, per_device(): lax.psum_scatter(grad_cquery.astype(jnp.bfloat16), 'rows', scatter_dimens...  183 us
    reduce_scatter x1, waiting for transfers between devices, per_device(): lax.psum_scatter(grad_squery.astype(jnp.bfloat16), 'rows', scatter_dimens...  183 us
    reduce_scatter x1, waiting for transfers between devices, per_device(): lax.psum_scatter(self_attention_key_gradient.astype(jnp.bfloat16), 'rows'...  183 us
    reduce_scatter x1, waiting for transfers between devices, per_device(): lax.psum_scatter(grad_sout.astype(jnp.bfloat16), 'rows', scatter_dimensio...  182 us
  transfers between devices with their start and end apart: 33, of which 30 were waited for; matrix products, arithmetic and copies ran while one was open for 5% of the time, Pallas kernels for 0%

commit v1 on v0

--- a/solution.py
+++ b/solution.py
@@ -8,6 +8,14 @@
 PER_ROW = 2
 CAP = 16
 EPSILON = 1e-05
+
+
+def _define_files(incoming_x, where_dim):
+    spare = jnp.concatenate(
+        lax.all_to_all(jnp.stack(lax.axis_size("rows") * [incoming_x], axis=0), "rows", 0, 0),
+        where_dim,
+    )
+    return spare
 
 
 def layer_stats(resid):
@@ -154,7 +162,7 @@
         lax.all_gather(self_value, "rows", axis=0, tiled=True),
         lax.all_gather(self_output, "rows", axis=1, tiled=True),
         lax.all_gather(cross_query, "rows", axis=0, tiled=True),
-        lax.all_gather(cross_key, "rows", axis=0, tiled=True),
+        _define_files(cross_key, 0),
         lax.all_gather(cross_value, "rows", axis=0, tiled=True),
         lax.all_gather(cross_output, "rows", axis=1, tiled=True),
         lax.all_gather(up_weight, "rows", axis=0, tiled=True),

time: 3420 us -> 3380 us (0.988)
  waiting for transfers between devices: 2740 us -> 2640 us
  blocking collectives: 385 us -> 434 us
    all_gather x1 -> x0, waiting for transfers between devices: 75.4 us -> none  [per_device(): lax.all_gather(cross_key, 'rows', axis=0, tiled=True)]
    all_gather x1, blocking collectives: 6 us -> 54.8 us  [per_device(): caption_full = lax.all_gather(caption_embed, 'text', axis=1, tiled=True)]
    unnamed x35 -> x34, waiting for transfers between devices: 383 us -> 382 us
  transfers between devices with their start and end apart: 33 -> 33, of which waited for: 30 -> 29; matrix products, arithmetic and copies ran while one was open for 5% -> 6% of each run, Pallas kernels for 0% -> 0%
where the time goes in v1:
time: 3380 us; the launch traced here: 3370 us
  waiting for transfers between devices  2640 us (78%)
  blocking collectives  434 us (13%)
  matrix products  169 us (5%)
  local copies, waits for them, and re-layouts  49.5 us (1%)
  other arithmetic  45.2 us (1%)
    unnamed x34, waiting for transfers between devices  382 us
    unnamed x2, blocking collectives  369 us
    reduce_scatter x1, waiting for transfers between devices, per_device(): lax.psum_scatter(grad_down.astype(jnp.bfloat16), 'rows', scatter_dimensio...  199 us
    reduce_scatter x1, waiting for transfers between devices, per_device(): lax.psum_scatter(grad_up.astype(jnp.bfloat16), 'rows', scatter_dimension=...  198 us
    reduce_scatter x1, waiting for transfers between devices, per_device(): lax.psum_scatter(self_attention_key_gradient.astype(jnp.bfloat16), 'rows'...  183 us
    reduce_scatter x1, waiting for transfers between devices, per_device(): lax.psum_scatter(grad_cquery.astype(jnp.bfloat16), 'rows', scatter_dimens...  183 us
    reduce_scatter x1, waiting for transfers between devices, per_device(): lax.psum_scatter(grad_sout.astype(jnp.bfloat16), 'rows', scatter_dimensio...  183 us
    reduce_scatter x1, waiting for transfers between devices, per_device(): lax.psum_scatter(grad_squery.astype(jnp.bfloat16), 'rows', scatter_dimens...  183 us
  transfers between devices with their start and end apart: 33, of which 29 were waited for; matrix products, arithmetic and copies ran while one was open for 6% of the time, Pallas kernels for 0%

profile of v1, /device:TPU:0, one launch (start us, length us, event | category | flops | bytes accessed | tf_op | source)
XLA Modules:
  0.0 3368.5 jit_solution(4046444457297018939)
XLA Ops:
  14.3 185.2 %all-reduce.8 = (bf16[2048]{0:T(1024)(128)(2,1)S(1)}, bf16[2048]{0:T(1024)(128)(2,1)S(1)}, bf16[2048]{0:T(1024)(128)(2,1)}) all-reduce(bf16[2048]{0:T(1024)(128)(2,1)S(1)} %dynamic-update-slice, bf16[2048]{0:T(1024)(128)(2,1)S(1)} %dynamic-update-slice.1, ...), channel_id=1, replica_groups=mesh['rows'=32,'text'=4] {'rows'}, use_global_device_ids=true, to_apply=%add | all-reduce | flops 6144 | bytes 24576
  204.5 20.8 all-gather.16.cloned.1.call-done
  225.3 75.0 %all-gather.20.cloned.1.call-done = bf16[2048,512]{1,0:T(8,128)(2,1)} async-done(((bf16[64,512]{1,0:T(8,128)(2,1)}), bf16[2048,512]{1,0:T(8,128)(2,1)}) %all-gather.20.cloned.1.call-update) | async-done | bytes 2097168 | tf_op jit(solution)/shard_map/all_gather | solution.py:160
  300.3 3.5 fusion.56
  304.1 68.2 %all-gather.22.cloned.1.call-done = bf16[2048,512]{1,0:T(8,128)(2,1)} async-done(((bf16[64,512]{1,0:T(8,128)(2,1)}), bf16[2048,512]{1,0:T(8,128)(2,1)}) %all-gather.22.cloned.1.call-update) | async-done | bytes 2097168 | tf_op jit(solution)/shard_map/all_gather | solution.py:161
  372.4 3.5 fusion.59
  376.3 68.1 %all-gather.18.cloned.1.call-done = bf16[2048,512]{1,0:T(8,128)(2,1)} async-done(((bf16[64,512]{1,0:T(8,128)(2,1)}), bf16[2048,512]{1,0:T(8,128)(2,1)}) %all-gather.18.cloned.1.call-update) | async-done | bytes 2097168 | tf_op jit(solution)/shard_map/all_gather | solution.py:162
  444.3 3.5 fusion.53
  451.3 65.0 %all-gather.24.cloned.1.call-done = bf16[512,2048]{0,1:T(8,128)(2,1)} async-done(((bf16[512,64]{0,1:T(8,128)(2,1)}), bf16[512,2048]{0,1:T(8,128)(2,1)}) %all-gather.24.cloned.1.call-update) | async-done | bytes 2097168 | tf_op jit(solution)/shard_map/all_gather | solution.py:163
  516.3 4.9 convolution_bitcast_fusion.1
  522.8 42.1 %reduce-scatter.22.cloned.1.call-done = f32[1,128,2048]{2,1,0:T(8,128)} async-done(((f32[1,512,2048]{2,1,0:T(8,128)}), f32[1,128,2048]{2,1,0:T(8,128)}) %reduce-scatter.22.cloned.1.call-update) | async-done | bytes 1048592 | tf_op jit(solution)/shard_map/reduce_scatter | solution.py:48
  570.2 9.7 all-to-all-start
  580.5 54.8 %all_gather.63 = bf16[1,32,4096]{2,1,0:T(8,128)(2,1)S(1)} all-gather(bf16[1,8,4096]{2,1,0:T(8,128)(2,1)S(1)} %copy-done.30), channel_id=1, replica_groups=mesh['rows'=32,'text'=4] {'text'}, dimensions={1}, use_global_device_ids=true | all-gather | bytes 327680 | tf_op jit(solution)/shard_map/all_gather | solution.py:185
  635.5 3.0 convolution_convert_fusion.16
  639.1 52.5 %all-gather.26.cloned.1.call-done = bf16[4096,512]{1,0:T(8,128)(2,1)} async-done(((bf16[128,512]{1,0:T(8,128)(2,1)}), bf16[4096,512]{1,0:T(8,128)(2,1)}) %all-gather.26.cloned.1.call-update) | async-done | bytes 4194320 | tf_op jit(solution)/shard_map/all_gather | solution.py:166
  691.6 3.0 convolution_convert_fusion.17
  695.2 69.6 %all-gather.30.cloned.1.call-done = bf16[2048,512]{1,0:T(8,128)(2,1)} async-done(((bf16[64,512]{1,0:T(8,128)(2,1)}), bf16[2048,512]{1,0:T(8,128)(2,1)}) %all-gather.30.cloned.1.call-update) | async-done | bytes 2097168 | tf_op jit(solution)/shard_map/all_gather | solution.py:164
  764.8 29.5 all-gather.28.cloned.1.call-done
  794.3 4.3 fusion.62
  807.1 62.5 %all-gather.32.cloned.1.call-done = bf16[512,2048]{0,1:T(8,128)(2,1)} async-done(((bf16[512,64]{0,1:T(8,128)(2,1)}), bf16[512,2048]{0,1:T(8,128)(2,1)}) %all-gather.32.cloned.1.call-update) | async-done | bytes 2097168 | tf_op jit(solution)/shard_map/all_gather | solution.py:167
  869.6 5.1 convolution_bitcast_fusion
  876.0 42.4 %reduce-scatter.24.cloned.1.call-done = f32[1,128,2048]{2,1,0:T(8,128)} async-done(((f32[1,512,2048]{2,1,0:T(8,128)}), f32[1,128,2048]{2,1,0:T(8,128)}) %reduce-scatter.24.cloned.1.call-update) | async-done | bytes 1048592 | tf_op jit(solution)/shard_map/reduce_scatter | solution.py:48
  923.5 102.7 %all-gather.36.cloned.1.call-done = bf16[2048,2048]{1,0:T(8,128)(2,1)} async-done(((bf16[64,2048]{1,0:T(8,128)(2,1)}), bf16[2048,2048]{1,0:T(8,128)(2,1)}) %all-gather.36.cloned.1.call-update) | async-done | bytes 8388624 | tf_op jit(solution)/shard_map/all_gather | solution.py:168
  1026.2 29.1 all-gather.34.cloned.1.call-done
  1055.3 18.3 multiply_convert_fusion
  1073.7 13.2 all-gather.40.cloned.1.call-done
  1086.8 107.9 %all-gather.38.cloned.1.call-done = bf16[2048,2048]{0,1:T(8,128)(2,1)} async-done(((bf16[2048,64]{0,1:T(8,128)(2,1)}), bf16[2048,2048]{0,1:T(8,128)(2,1)}) %all-gather.38.cloned.1.call-update) | async-done | bytes 8388624 | tf_op jit(solution)/shard_map/all_gather | solution.py:169
  1194.8 12.0 add_convert_fusion.1
  1208.2 6.2 fusion.10
  1214.5 10.5 convolution_bitcast_fusion.2
  1225.1 15.6 reduce-scatter.28.cloned.1.call-done
  1243.6 45.8 %reduce-scatter.26.cloned.1.call-done = f32[1,128,2048]{2,1,0:T(8,128)} async-done(((f32[1,512,2048]{2,1,0:T(8,128)}), f32[1,128,2048]{2,1,0:T(8,128)}) %reduce-scatter.26.cloned.1.call-update) | async-done | bytes 1048592 | tf_op jit(solution)/shard_map/reduce_scatter | solution.py:48
  1289.4 3.9 fusion.171
  1294.1 29.3 all-gather.42.cloned.1.call-done
  1323.4 4.3 fusion.65
  1336.2 4.4 fusion.12
  1340.7 29.3 reduce-scatter.30.cloned.1.call-done
  1372.1 3.0 fusion.169
  1378.1 3.6 fusion.155
  1383.8 4.4 convolution_convert_fusion.4
  1388.3 4.2 convolution_convert_fusion.5
  1392.6 10.1 convolution_convert_fusion
  1403.0 10.0 convolution_convert_fusion.1
  1413.1 3.3 fusion.1
  1416.4 6.5 copy.121
  1423.7 3.3 fusion
  1427.0 6.6 copy.119
  1434.6 4.3 convolution_convert_fusion.6
  1439.2 3.5 fusion.68
  1449.6 4.4 convolution_convert_fusion.8
  1458.3 4.3 convolution_convert_fusion.9
  1465.4 3.0 fusion.107
  1477.7 139.2 %reduce-scatter.46.cloned.1.call-done = bf16[512,64]{0,1:T(8,128)(2,1)} async-done(((bf16[512,2048]{0,1:T(8,128)(2,1)}), bf16[512,64]{0,1:T(8,128)(2,1)}) %reduce-scatter.46.cloned.1.call-update) | async-done | bytes 65552 | tf_op jit(solution)/shard_map/reduce_scatter | solution.py:296
  1618.5 183.0 %reduce-scatter.44.cloned.1.call-done = bf16[64,512]{1,0:T(8,128)(2,1)} async-done(((bf16[2048,512]{1,0:T(8,128)(2,1)}), bf16[64,512]{1,0:T(8,128)(2,1)}) %reduce-scatter.44.cloned.1.call-update) | async-done | bytes 65552 | tf_op jit(solution)/shard_map/reduce_scatter | solution.py:287
  1803.0 199.0 %reduce-scatter.50.cloned.1.call-done = bf16[2048,64]{0,1:T(8,128)(2,1)} async-done(((bf16[2048,2048]{0,1:T(8,128)(2,1)}), bf16[2048,64]{0,1:T(8,128)(2,1)}) %reduce-scatter.50.cloned.1.call-update) | async-done | bytes 262160 | tf_op jit(solution)/shard_map/reduce_scatter | solution.py:302
  2003.7 198.2 %reduce-scatter.48.cloned.1.call-done = bf16[64,2048]{1,0:T(8,128)(2,1)} async-done(((bf16[2048,2048]{1,0:T(8,128)(2,1)}), bf16[64,2048]{1,0:T(8,128)(2,1)}) %reduce-scatter.48.cloned.1.call-update) | async-done | bytes 262160 | tf_op jit(solution)/shard_map/reduce_scatter | solution.py:299
  2203.7 188.1 %reduce-scatter.54.cloned.1.call-done = bf16[128,512]{1,0:T(8,128)(2,1)} async-done(((bf16[4096,512]{1,0:T(8,128)(2,1)}), bf16[128,512]{1,0:T(8,128)(2,1)}) %reduce-scatter.54.cloned.1.call-update) | async-done | bytes 131088
  2393.6 187.7 %reduce-scatter.52.cloned.1.call-done = bf16[128,512]{1,0:T(8,128)(2,1)} async-done(((bf16[4096,512]{1,0:T(8,128)(2,1)}), bf16[128,512]{1,0:T(8,128)(2,1)}) %reduce-scatter.52.cloned.1.call-update) | async-done | bytes 131088
  2583.1 182.7 %reduce-scatter.42.cloned.1.call-done = bf16[512,64]{0,1:T(8,128)(2,1)} async-done(((bf16[512,2048]{0,1:T(8,128)(2,1)}), bf16[512,64]{0,1:T(8,128)(2,1)}) %reduce-scatter.42.cloned.1.call-update) | async-done | bytes 65552 | tf_op jit(solution)/shard_map/reduce_scatter | solution.py:284
  2767.4 183.1 %reduce-scatter.38.cloned.1.call-done = bf16[64,512]{1,0:T(8,128)(2,1)} async-done(((bf16[2048,512]{1,0:T(8,128)(2,1)}), bf16[64,512]{1,0:T(8,128)(2,1)}) %reduce-scatter.38.cloned.1.call-update) | async-done | bytes 65552 | tf_op jit(solution)/shard_map/reduce_scatter | solution.py:275
  2952.0 182.6 %reduce-scatter.36.cloned.1.call-done = bf16[64,512]{1,0:T(8,128)(2,1)} async-done(((bf16[2048,512]{1,0:T(8,128)(2,1)}), bf16[64,512]{1,0:T(8,128)(2,1)}) %reduce-scatter.36.cloned.1.call-update) | async-done | bytes 65552 | tf_op jit(solution)/shard_map/reduce_scatter | solution.py:272
  3136.1 24.0 reduce-scatter.32.cloned.1.call-done
  3161.6 10.3 all-reduce.6
  3171.9 183.9 %all-reduce.7 = (bf16[2048]{0:T(1024)(128)(2,1)S(1)}, bf16[2048]{0:T(1024)(128)(2,1)S(1)}, bf16[2048]{0:T(1024)(128)(2,1)S(1)}) all-reduce(bf16[2048]{0:T(1024)(128)(2,1)S(1)} %get-tuple-element.73, bf16[2048]{0:T(1024)(128)(2,1)S(1)} %get-tuple-element.74, ...), channel_id=9, replica_groups=mesh['rows'=32,'text'=4] {'rows'}, use_global_device_ids=true, to_apply=%region_27.28.clone | all-reduce | flops 6144 | bytes 24576
  (257 shorter events, 107.1 us)
Async XLA Ops:
  7.2 218.1 %all-gather.16.cloned.1.call-start = ((), (), s32[]{:S(2)}) async-start(), calls=%async_computation.18 | async-start | bytes 2621440 | tf_op jit(solution)/shard_map/all_gather | solution.py:44
  8.4 216.9 %copy-start.37 = (f32[128]{0:T(128)}, f32[128]{0:T(128)S(1)}, u32[]{:S(2)}) copy-start(f32[128]{0:T(128)S(1)} %broadcast_multiply_fusion.8) | copy-start | bytes 1540
  9.8 215.5 %copy-start.41 = (f32[128]{0:T(128)}, f32[128]{0:T(128)S(1)}, u32[]{:S(2)}) copy-start(f32[128]{0:T(128)S(1)} %add_rsqrt_fusion.2) | copy-start | bytes 1540
  199.5 25.8 copy-start.23
  201.8 98.5 %all-gather.20.cloned.1.call-start = ((), (), s32[]{:S(2)}) async-start(), calls=%async_computation.20 | async-start | bytes 2162688 | tf_op jit(solution)/shard_map/all_gather | solution.py:160
  202.5 169.9 %all-gather.22.cloned.1.call-start = ((), (), s32[]{:S(2)}) async-start(), calls=%async_computation.21 | async-start | bytes 2162688 | tf_op jit(solution)/shard_map/all_gather | solution.py:161
  203.3 241.1 %all-gather.18.cloned.1.call-start = ((), (), s32[]{:S(2)}) async-start(), calls=%async_computation.19 | async-start | bytes 2162688 | tf_op jit(solution)/shard_map/all_gather | solution.py:162
  203.8 312.5 %all-gather.24.cloned.1.call-start = ((), (), s32[]{:S(2)}) async-start(), calls=%async_computation.22 | async-start | bytes 2162688 | tf_op jit(solution)/shard_map/all_gather | solution.py:163
  204.4 360.5 %reduce-scatter.22.cloned.1.call-start = ((), (), s32[]{:S(2)}) async-start(), calls=%async_computation.23 | async-start | bytes 5242880 | tf_op jit(solution)/shard_map/reduce_scatter | solution.py:48
  304.1 144.6 %copy-start.6 = (bf16[2,256,4,128]{1,3,2,0:T(8,128)(2,1)}, bf16[2,256,4,128]{1,3,2,0:T(8,128)(2,1)S(1)}, u32[]{:S(2)}) copy-start(bf16[2,256,4,128]{1,3,2,0:T(8,128)(2,1)S(1)} %copy.103) | copy-start | bytes 1572868
  376.3 72.5 %copy-start.5 = (bf16[2,256,4,128]{1,3,2,0:T(8,128)(2,1)}, bf16[2,256,4,128]{1,3,2,0:T(8,128)(2,1)S(1)}, u32[]{:S(2)}) copy-start(bf16[2,256,4,128]{1,3,2,0:T(8,128)(2,1)S(1)} %copy.100) | copy-start | bytes 1572868
  451.3 69.8 %copy-start.17 = (bf16[1,2,256,4,128]{4,3,2,1,0:T(4,128)(2,1)}, bf16[1,2,256,4,128]{4,3,2,1,0:T(4,128)(2,1)S(1)}, u32[]{:S(2)}) copy-start(bf16[1,2,256,4,128]{4,3,2,1,0:T(4,128)(2,1)S(1)} %copy.89) | copy-start | bytes 1572868
  521.2 46.6 %copy-start.25 = (bf16[128,512]{1,0:T(8,128)(2,1)S(1)}, bf16[128,512]{1,0:T(8,128)(2,1)}, u32[]{:S(2)}) copy-start(bf16[128,512]{1,0:T(8,128)(2,1)} %param.29) | copy-start | bytes 393220
  521.2 170.4 %all-gather.26.cloned.1.call-start = ((), (), s32[]{:S(2)}) async-start(), calls=%async_computation.24 | async-start | bytes 4325376 | tf_op jit(solution)/shard_map/all_gather | solution.py:166
  521.9 242.8 %all-gather.30.cloned.1.call-start = ((), (), s32[]{:S(2)}) async-start(), calls=%async_computation.26 | async-start | bytes 2162688 | tf_op jit(solution)/shard_map/all_gather | solution.py:164
  522.7 271.6 %all-gather.28.cloned.1.call-start = ((), (), s32[]{:S(2)}) async-start(), calls=%async_computation.25 | async-start | bytes 2621440 | tf_op jit(solution)/shard_map/all_gather | solution.py:44
  566.4 3.8 copy-start.39
  566.7 3.5 copy-start.43
  570.2 10.3 copy-start.30
  570.2 65.2 %copy-start.46 = (s32[1,2]{1,0:T(1,128)S(1)}, s32[1,2]{1,0:T(1,128)}, u32[]{:S(2)}) copy-start(s32[1,2]{1,0:T(1,128)} %param.19) | copy-start | bytes 28
  570.2 65.2 %all-to-all-start = ((bf16[32,128,512]{2,1,0:T(8,128)(2,1)}), bf16[32,128,512]{2,1,0:T(8,128)(2,1)}, u32[]{:S(2)}, u32[]{:S(2)}) async-start(bf16[32,128,512]{2,1,0:T(8,128)(2,1)} %stack.2), calls=%async_computation.1 | async-start | bytes 8388608 | tf_op jit(solution)/shard_map/all_to_all | solution.py:15
  579.9 289.7 %all-gather.32.cloned.1.call-start = ((), (), s32[]{:S(2)}) async-start(), calls=%async_computation.27 | async-start | bytes 2162688 | tf_op jit(solution)/shard_map/all_gather | solution.py:167
  580.5 337.9 %reduce-scatter.24.cloned.1.call-start = ((), (), s32[]{:S(2)}) async-start(), calls=%async_computation.28 | async-start | bytes 5242880 | tf_op jit(solution)/shard_map/reduce_scatter | solution.py:48
  635.4 166.5 %copy-start.36 = (pred[2,16]{1,0:T(4,128)(4,1)}, pred[2,16]{1,0:T(4,128)(4,1)S(1)}, u32[]{:S(2)}) copy-start(pred[2,16]{1,0:T(4,128)(4,1)S(1)} %iota_compare_fusion) | copy-start | bytes 100
  874.7 151.5 %all-gather.36.cloned.1.call-start = ((), (), s32[]{:S(2)}) async-start(), calls=%async_computation.30 | async-start | bytes 8650752 | tf_op jit(solution)/shard_map/all_gather | solution.py:168
  875.3 180.1 %all-gather.34.cloned.1.call-start = ((), (), s32[]{:S(2)}) async-start(), calls=%async_computation.29 | async-start | bytes 2621440 | tf_op jit(solution)/shard_map/all_gather | solution.py:44
  922.3 164.6 %all-gather.40.cloned.1.call-start = ((), (), s32[]{:S(2)}) async-start(), calls=%async_computation.33 | async-start | bytes 2621440 | tf_op jit(solution)/shard_map/all_gather | solution.py:52
  922.9 271.9 %all-gather.38.cloned.1.call-start = ((), (), s32[]{:S(2)}) async-start(), calls=%async_computation.31 | async-start | bytes 8650752 | tf_op jit(solution)/shard_map/all_gather | solution.py:169
  923.5 317.3 %reduce-scatter.28.cloned.1.call-start = ((), (), s32[]{:S(2)}) async-start(), calls=%async_computation.34 | async-start | bytes 2621440 | tf_op jit(solution)/shard_map/reduce_scatter | solution.py:56
  1194.8 13.4 copy-start.44
  1214.4 75.0 %reduce-scatter.26.cloned.1.call-start = ((), (), s32[]{:S(2)}) async-start(), calls=%async_computation.32 | async-start | bytes 5242880 | tf_op jit(solution)/shard_map/reduce_scatter | solution.py:48
  1225.0 98.4 %all-gather.42.cloned.1.call-start = ((), (), s32[]{:S(2)}) async-start(), calls=%async_computation.35 | async-start | bytes 2621440 | tf_op jit(solution)/shard_map/all_gather | solution.py:52
  1293.4 76.7 %reduce-scatter.30.cloned.1.call-start = ((), (), s32[]{:S(2)}) async-start(), calls=%async_computation.36 | async-start | bytes 2621440 | tf_op jit(solution)/shard_map/reduce_scatter | solution.py:56
  1340.6 93.0 %all-gather.44.cloned.1.call-start = ((), (), s32[]{:S(2)}) async-start(), calls=%async_computation.37 | async-start | bytes 2621440 | tf_op jit(solution)/shard_map/all_gather | solution.py:52
  1375.1 101.1 %reduce-scatter.34.cloned.1.call-start = ((), (), s32[]{:S(2)}) async-start(), calls=%async_computation.39 | async-start | bytes 327680 | tf_op jit(solution)/shard_map/reduce_scatter | solution.py:229
  1375.4 6.4 copy-start.2
  1376.8 4.9 copy-start.21
  1378.1 5.7 copy-start.19
  1383.8 4.5 copy-start.20
  1383.8 233.2 %reduce-scatter.46.cloned.1.call-start = ((), (), s32[]{:S(2)}) async-start(), calls=%async_computation.45 | async-start | bytes 2162688 | tf_op jit(solution)/shard_map/reduce_scatter | solution.py:296
  1388.3 413.2 %reduce-scatter.44.cloned.1.call-start = ((), (), s32[]{:S(2)}) async-start(), calls=%async_computation.44 | async-start | bytes 2162688 | tf_op jit(solution)/shard_map/reduce_scatter | solution.py:287
  1392.5 609.4 %reduce-scatter.50.cloned.1.call-start = ((), (), s32[]{:S(2)}) async-start(), calls=%async_computation.47 | async-start | bytes 8650752 | tf_op jit(solution)/shard_map/reduce_scatter | solution.py:302
  1402.7 799.2 %reduce-scatter.48.cloned.1.call-start = ((), (), s32[]{:S(2)}) async-start(), calls=%async_computation.46 | async-start | bytes 8650752 | tf_op jit(solution)/shard_map/reduce_scatter | solution.py:299
  1413.0 978.7 %reduce-scatter.54.cloned.1.call-start = ((), (), s32[]{:S(2)}) async-start(), calls=%async_computation.49 | async-start | bytes 4325376
  1422.9 1158.4 %reduce-scatter.52.cloned.1.call-start = ((), (), s32[]{:S(2)}) async-start(), calls=%async_computation.48 | async-start | bytes 4325376
  1433.5 5.6 copy-start.27
  1433.6 5.6 copy-start.32
  1433.6 1332.3 %reduce-scatter.42.cloned.1.call-start = ((), (), s32[]{:S(2)}) async-start(), calls=%async_computation.43 | async-start | bytes 2162688 | tf_op jit(solution)/shard_map/reduce_scatter | solution.py:284
  1438.8 1511.6 %reduce-scatter.38.cloned.1.call-start = ((), (), s32[]{:S(2)}) async-start(), calls=%async_computation.41 | async-start | bytes 2162688 | tf_op jit(solution)/shard_map/reduce_scatter | solution.py:275
  1439.2 5.7 copy-start.14
  1454.0 1680.6 %reduce-scatter.36.cloned.1.call-start = ((), (), s32[]{:S(2)}) async-start(), calls=%async_computation.40 | async-start | bytes 2162688 | tf_op jit(solution)/shard_map/reduce_scatter | solution.py:272
  1458.3 4.4 copy-start.4
  1462.6 2.8 copy-start.9
  1462.6 1697.5 %reduce-scatter.32.cloned.1.call-start = ((), (), s32[]{:S(2)}) async-start(), calls=%async_computation.38 | async-start | bytes 2621440 | tf_op jit(solution)/shard_map/reduce_scatter | solution.py:56
  1465.4 3.1 copy-start.11
  1465.4 3.1 copy-start.15
  1472.7 1884.8 %reduce-scatter.40.cloned.1.call-start = ((), (), s32[]{:S(2)}) async-start(), calls=%async_computation.42 | async-start | bytes 2162688 | tf_op jit(solution)/shard_map/reduce_scatter | solution.py:281
  1475.4 1684.7 %copy-start.1 = (bf16[1,128,2048]{2,1,0:T(8,128)(2,1)S(1)}, bf16[1,128,2048]{2,1,0:T(8,128)(2,1)}, u32[]{:S(2)}) copy-start(bf16[1,128,2048]{2,1,0:T(8,128)(2,1)} %param.17) | copy-start | bytes 1572868
  1475.4 1684.7 %copy-start.24 = (f32[2048]{0:T(1024)S(1)}, f32[2048]{0:T(1024)}, u32[]{:S(2)}) copy-start(f32[2048]{0:T(1024)} %copy-done.23) | copy-start | bytes 24580
  1475.4 1684.7 %copy-start.38 = (f32[128]{0:T(128)S(1)}, f32[128]{0:T(128)}, u32[]{:S(2)}) copy-start(f32[128]{0:T(128)} %copy-done.37) | copy-start | bytes 1540
  1475.4 1684.7 %copy-start.42 = (f32[128]{0:T(128)S(1)}, f32[128]{0:T(128)}, u32[]{:S(2)}) copy-start(f32[128]{0:T(128)} %copy-done.41) | copy-start | bytes 1540
  1475.4 1686.2 %copy-start.33 = (f32[2048]{0:T(1024)S(1)}, f32[2048]{0:T(1024)}, u32[]{:S(2)}) copy-start(f32[2048]{0:T(1024)} %get-tuple-element.64) | copy-start | bytes 24580
  1475.4 1686.2 %copy-start.34 = (f32[2048]{0:T(1024)S(1)}, f32[2048]{0:T(1024)}, u32[]{:S(2)}) copy-start(f32[2048]{0:T(1024)} %get-tuple-element.66) | copy-start | bytes 24580
  1475.4 1883.6 %copy-start.8 = (f32[1,128,2048]{2,1,0:T(8,128)S(1)}, f32[1,128,2048]{2,1,0:T(8,128)}, u32[]{:S(2)}) copy-start(f32[1,128,2048]{2,1,0:T(8,128)} %get-tuple-element.83) | copy-start | bytes 3145732
  (17 other events, 17.6 us)
Sparse Core Ops, SparseCore 0:
  201.9 23.3 all-gather.15
  228.5 71.7 all-gather.19
  303.4 68.9 all-gather.21
  375.4 68.9 all-gather.17
  447.4 68.9 all-gather.23
  521.3 43.5 reduce-scatter.21
  568.5 123.0 all-gather.25
  695.2 69.5 all-gather.29
  767.1 27.1 all-gather.27
  797.8 71.7 all-gather.31
  874.8 43.5 reduce-scatter.23
  921.4 104.7 all-gather.35
  1028.4 26.8 all-gather.33
  1056.8 29.9 all-gather.39
  1089.9 104.8 all-gather.37
  1214.5 26.1 reduce-scatter.27
  1243.1 46.2 reduce-scatter.25
  1293.5 29.8 all-gather.41
  1340.7 29.2 reduce-scatter.29
  1375.3 29.8 all-gather.43
  1408.2 18.2 reduce-scatter.33
  1428.9 187.9 reduce-scatter.45
  1619.5 181.9 reduce-scatter.43
  1803.7 198.1 reduce-scatter.49
  2004.4 197.5 reduce-scatter.47
  2204.2 187.5 reduce-scatter.53
  2394.0 187.2 reduce-scatter.51
  2583.7 182.1 reduce-scatter.41
  2768.4 182.0 reduce-scatter.37
  2952.7 181.8 reduce-scatter.35
  3137.1 22.9 reduce-scatter.31
  3162.5 188.2 reduce-scatter.39
